TPU v7x, 768 devices: a whole 4x8x12 slice. The times are simulated.
768 devices in a mesh: dom: 192 (over y, z, core), sub: 4 (over x).
Axes of the slice: x: 4, y: 8, z: 12, core: 2. Of those that a mesh axis runs over, the one named last changes fastest.
Arguments:
- section_state: float32 [6144, 5, 128], P(('dom', 'sub')), may hold values from -2.5 to 10, as said below
- base_state: float32 [6144, 5, 128], P(('dom', 'sub')), may hold values from -2.5 to 10, as said below
- pseudo_interval_ratio: float32 [6144, 128], P(('dom', 'sub')), may hold values from 0.1 to 0.4
- send_list: int32 [192, 4, 4, 4], P('dom', 'sub'), may hold values from -1 to 7, as said below
- face_tiles: bfloat16 [24576, 3, 128, 128], P(('dom', 'sub')), may hold values from -0.15625 to 0.15625
- tile_row: int32 [24576], P(('dom', 'sub')), may hold values from 0 to 31, as said below
- tile_col: int32 [24576], P(('dom', 'sub')), may hold values from 0 to 95, as said below
- tile_flip: int32 [24576], P(('dom', 'sub')), may hold values 0 or 1
Outputs:
- updated_state: float32 [6144, 5, 128], P(('dom', 'sub'))
Inputs may be any that keep to these rules, and one draw needn't show every extreme that they name: `send_list`: in each list the first entries (one to 4 of them) name distinct blocks of the sending device; the others are -1. One list of every partition has all 4 entries, and so does the list of every partition's last sub-partition for offset -2. `tile_row`: every block of a partition owns exactly 4 of the partition's tiles. `tile_col`: A tile's column is an own block of its partition (below 32) or a ghost slot whose sending partition exists on the curve (0 <= q < 192) and whose list entry is not -1. `section_state`: density and pressure lie in 0.5 to 2 in every cell; energy = pressure / 0.4 + 0.5 |momentum|^2 / density. `base_state`: density and pressure lie in 0.5 to 2 in every cell; energy = pressure / 0.4 + 0.5 |momentum|^2 / density.
All inputs are finite; a program needn't handle non-finite values. No bound on the sum of `tile_flip` on one device may be relied on, other than what follows from the above.
Results may differ from a plain program's by a relative error of at most 0.00042.
Values sent between devices are 32-bit elements; how exact they have to be, the bound alone decides.
A program may use at most 32 MiB of HBM per device.

v0:
```python
import jax
import jax.numpy as jnp
from jax import lax
from jax.sharding import PartitionSpec as P

gamma_gas = 1.4
viscosity = 0.3
conductivity = 1.46
smoothing = 0.1
section_coef = 0.5
curve_steps = (1, -1, 2, -2)


def shifted(value, axis, steps):
    count = lax.axis_size(axis)
    pairs = [(source, (source + steps) % count) for source in range(count)]
    return lax.ppermute(value, axis, pairs)


def primitives(conserved):
    gas_rho_field = conserved[:, 0]
    momentum = conserved[:, 1:4]
    velocity = momentum / gas_rho_field[:, None]
    normal_load_field = (gamma_gas - 1.0) * (
        conserved[:, 4] - 0.5 * jnp.sum(momentum * velocity, axis=1)
    )
    return (gas_rho_field, velocity, normal_load_field)


def convective(conserved, velocity, normal_load_field):
    momentum = conserved[:, 1:4]
    identity = jnp.eye(3, dtype=jnp.float32)
    moment_flux = (
        momentum[:, None, :, :] * velocity[:, :, None, :]
        + normal_load_field[:, None, None, :] * identity[None, :, :, None]
    )
    energy_flux = (conserved[:, 4] + normal_load_field)[:, None, :] * velocity
    return jnp.concatenate(
        [momentum[:, :, None, :], moment_flux, energy_flux[:, :, None, :]], axis=2
    )


def viscous(gas_rho_field, velocity, normal_load_field, received_gradient_rows):
    shear = received_gradient_rows[:, :, 1:4]
    divergence = shear[:, 0, 0] + shear[:, 1, 1] + shear[:, 2, 2]
    identity = jnp.eye(3, dtype=jnp.float32)
    stress = viscosity * (
        shear
        + jnp.swapaxes(shear, 1, 2)
        - 2.0 / 3.0 * divergence[:, None, None, :] * identity[None, :, :, None]
    )
    heat_level_field = normal_load_field / gas_rho_field
    heat_gradient = (
        received_gradient_rows[:, :, 4]
        - heat_level_field[:, None, :] * received_gradient_rows[:, :, 0]
    ) / gas_rho_field[:, None, :]
    work_flux = jnp.sum(stress * velocity[:, None, :, :], axis=2) + conductivity * heat_gradient
    starting_rho_field = jnp.zeros_like(work_flux)[:, :, None, :]
    return jnp.concatenate([starting_rho_field, stress, work_flux[:, :, None, :]], axis=2)


def wave_speed(gas_rho_field, velocity, normal_load_field):
    return jnp.sqrt(
        jnp.sum(velocity * velocity, axis=1) + gamma_gas * normal_load_field / gas_rho_field
    )


def per_device(
    section_state,
    base_state,
    pseudo_interval_ratio,
    send_list,
    face_tiles,
    tile_row,
    tile_col,
    tile_flip,
):
    blocks = section_state.shape[0]
    cells = section_state.shape[2]
    partition = blocks * lax.axis_size("sub")
    tile_count = face_tiles.shape[0]
    picked = jnp.maximum(send_list[0, 0], 0)

    def ghost_packets(values_in):
        packets = values_in[picked]
        arrived = []
        for number in range(len(curve_steps)):
            arrived.append(shifted(packets[number], "dom", curve_steps[number]))
        return jnp.stack(arrived)[:, None]

    def share_partition(values_in):
        owned, ghosts = (
            lax.all_gather(values_in, "sub", axis=0, tiled=True),
            lax.all_gather(ghost_packets(values_in), "sub", axis=1, tiled=True),
        )
        return jnp.concatenate([owned, ghosts.reshape((-1,) + values_in.shape[1:])], axis=0)

    def reduce_rows(partial_sum):
        return lax.psum_scatter(partial_sum, "sub", scatter_dimension=0, tiled=True)

    oriented = jnp.where(
        tile_flip[:, None, None, None] == 1, -jnp.swapaxes(face_tiles, 2, 3), face_tiles
    )
    owners = (jnp.arange(partition, dtype=jnp.int32)[:, None] == tile_row[None, :]).astype(
        jnp.float32
    )
    ext_state = share_partition(section_state)
    columns = ext_state[tile_col]
    row_state = ext_state[tile_row]
    gas_rho_field, velocity, normal_load_field = primitives(columns)
    prim_cols = jnp.concatenate(
        [gas_rho_field[:, None], velocity, normal_load_field[:, None]], axis=1
    ).astype(jnp.bfloat16)
    terms = jnp.einsum("tdab,tvb->tdva", oriented, prim_cols, preferred_element_type=jnp.float32)
    partial_slopes = jnp.dot(
        owners, terms.reshape(tile_count, -1), precision=lax.Precision.HIGHEST
    ).reshape(partition, 15, cells)
    ext_slopes = share_partition(reduce_rows(partial_slopes))
    col_slopes = ext_slopes[tile_col].reshape(tile_count, 3, 5, cells)
    fluxes = (
        convective(columns, velocity, normal_load_field)
        - viscous(gas_rho_field, velocity, normal_load_field, col_slopes)
    ).astype(jnp.bfloat16)
    scaled = (wave_speed(gas_rho_field, velocity, normal_load_field)[:, None, :] * columns).astype(
        jnp.bfloat16
    )
    row_density, row_velocity, row_pressure = primitives(row_state)
    row_scaled = wave_speed(row_density, row_velocity, row_pressure)[:, None, :] * row_state
    absolute = jnp.sum(jnp.abs(oriented), axis=1, dtype=jnp.float32).astype(jnp.bfloat16)
    flux_sum = jnp.einsum("tdab,tdvb->tva", oriented, fluxes, preferred_element_type=jnp.float32)
    spread = jnp.einsum("tab,tvb->tva", absolute, scaled, preferred_element_type=jnp.float32)
    spread = spread - jnp.sum(absolute, axis=2, dtype=jnp.float32)[:, None, :] * row_scaled
    contribution = flux_sum - smoothing * spread
    partial_residual = jnp.dot(
        owners, contribution.reshape(tile_count, -1), precision=lax.Precision.HIGHEST
    ).reshape(partition, 5, cells)
    residual = reduce_rows(partial_residual)
    return base_state - section_coef * pseudo_interval_ratio[:, None, :] * residual


def solution(mesh):
    return jax.shard_map(
        per_device,
        mesh=mesh,
        in_specs=(
            P(("dom", "sub"), None, None),
            P(("dom", "sub"), None, None),
            P(("dom", "sub"), None),
            P("dom", "sub", None, None),
            P(("dom", "sub"), None, None, None),
            P(("dom", "sub")),
            P(("dom", "sub")),
            P(("dom", "sub")),
        ),
        out_specs=P(("dom", "sub"), None, None),
        check_vma=False,
    )
```

profile of v0, /device:TPU:8, one launch (start us, length us, event | category | flops | bytes accessed | tf_op | source)
XLA Modules:
  0.0 188.5 jit_solution(1105823272584547359)
XLA Ops:
  8.7 1.9 %collective-permute-start = (f32[4,5,128]{2,0,1:T(4,128)S(1)}, f32[4,5,128]{2,0,1:T(4,128)S(1)}, u32[]{:S(2)}, u32[]{:S(2)}) collective-permute-start(f32[4,5,128]{2,0,1:T(4,128)S(1)} %get-tuple-element.29), channel_id=1, source_target_pairs={{0,4},{4,8},{8,12},{12,16},{16,20},{20,24},{24,28},{28,32},{32,36}... | collective-permute-start | bytes 30728 | tf_op jit(solution)/shard_map/ppermute | solution.py:17
  10.6 4.3 %collective-permute-start.2 = (f32[4,5,128]{2,0,1:T(4,128)S(1)}, f32[4,5,128]{2,0,1:T(4,128)S(1)}, u32[]{:S(2)}, u32[]{:S(2)}) collective-permute-start(f32[4,5,128]{2,0,1:T(4,128)S(1)} %get-tuple-element.30), channel_id=1, source_target_pairs={{0,8},{4,12},{8,16},{12,20},{16,24},{20,28},{24,32},{28,36},{32,40... | collective-permute-start | bytes 30728 | tf_op jit(solution)/shard_map/ppermute | solution.py:17
  14.9 11.6 %collective-permute-start.1 = (f32[4,5,128]{2,0,1:T(4,128)S(1)}, f32[4,5,128]{2,0,1:T(4,128)S(1)}, u32[]{:S(2)}, u32[]{:S(2)}) collective-permute-start(f32[4,5,128]{2,0,1:T(4,128)S(1)} %get-tuple-element.31), channel_id=1, source_target_pairs={{0,764},{4,0},{8,4},{12,8},{16,12},{20,16},{24,20},{28,24},{32,28}... | collective-permute-start | bytes 30728 | tf_op jit(solution)/shard_map/ppermute | solution.py:17
  26.5 4.2 %collective-permute-start.3 = (f32[4,5,128]{2,0,1:T(4,128)S(1)}, f32[4,5,128]{2,0,1:T(4,128)S(1)}, u32[]{:S(2)}, u32[]{:S(2)}) collective-permute-start(f32[4,5,128]{2,0,1:T(4,128)S(1)} %get-tuple-element.32), channel_id=1, source_target_pairs={{0,760},{4,764},{8,0},{12,4},{16,8},{20,12},{24,16},{28,20},{32,24... | collective-permute-start | bytes 30728 | tf_op jit(solution)/shard_map/ppermute | solution.py:17
  33.3 4.7 %copy.130 = bf16[32,3,128,128]{2,3,1,0:T(8,128)(2,1)} copy(bf16[32,3,128,128]{3,2,1,0:T(8,128)(2,1)} %param.12) | data formatting | bytes 6291456 | tf_op args[4]
  37.9 5.1 %abs_reduce_fusion = (bf16[32,128,128]{2,1,0:T(8,128)(2,1)S(1)}, bf16[32,3,128,128]{3,2,1,0:T(8,128)(2,1)S(1)}) fusion(bf16[32,3,128,128]{3,2,1,0:T(8,128)(2,1)} %param.12, bf16[32,3,128,128]{2,3,1,0:T(8,128)(2,1)} %copy.130, pred[32]{0:T(512)(128)(4,1)S(1)} %broadcast_compare_fusion), kind=kLoop, calls=%fused_computation.6 | loop fusion | flops 5767168 | bytes 10485792 | tf_op jit(solution)/shard_map/reduce_sum | solution.py:129
  44.1 12.2 %all_gather.12 = f32[32,5,128]{2,0,1:T(8,128)S(1)} all-gather(f32[8,5,128]{2,0,1:T(8,128)S(1)} %copy-done), channel_id=1, replica_groups=mesh['dom'=192,'sub'=4] {'sub'}, dimensions={0}, use_global_device_ids=true | all-gather | bytes 102400 | tf_op jit(solution)/shard_map/all_gather | solution.py:93
  57.0 12.1 %all-gather = f32[4,16,5,128]{3,0,2,1:T(4,128)S(1)} all-gather(f32[4,4,5,128]{3,0,2,1:T(4,128)S(1)} %copy.118), channel_id=2, replica_groups=mesh['dom'=192,'sub'=4] {'sub'}, dimensions={1}, use_global_device_ids=true | all-gather | bytes 204800 | tf_op jit(solution)/shard_map/all_gather | solution.py:94
  71.2 1.6 gather_fusion.1
  72.8 1.6 fusion.37
  78.6 1.9 %fusion.2 = f32[32,15,128]{2,0,1:T(8,128)} fusion(s32[32]{0:T(128)} %param.13, f32[32,1920]{1,0:T(8,128)} %reshape.83), kind=kOutput, calls=%fused_computation.15 | convolution fusion | flops 23593984 | bytes 491648 | tf_op jit(solution)/shard_map/dot_general | solution.py:115
  81.6 1.5 copy.124
  83.0 1.5 copy.138
  84.5 1.5 copy.126
  86.0 1.5 copy.122
  91.6 13.0 %reduce-scatter.3.cloned.1.call-done = f32[8,15,128]{2,0,1:T(8,128)} async-done(((f32[32,15,128]{2,0,1:T(8,128)}), f32[8,15,128]{2,0,1:T(8,128)}) %reduce-scatter.3.cloned.1.call-update) | async-done | bytes 61456 | tf_op jit(solution)/shard_map/reduce_scatter | solution.py:99
  106.1 1.9 %collective-permute-start.4 = (f32[4,15,128]{2,1,0:T(8,128)S(1)}, f32[4,15,128]{2,1,0:T(8,128)S(1)}, u32[]{:S(2)}, u32[]{:S(2)}) collective-permute-start(f32[4,15,128]{2,1,0:T(8,128)S(1)} %get-tuple-element.17), channel_id=1, source_target_pairs={{0,4},{4,8},{8,12},{12,16},{16,20},{20,24},{24,28},{28,32},{32,36}... | collective-permute-start | bytes 92168 | tf_op jit(solution)/shard_map/ppermute | solution.py:17
  108.0 3.5 %collective-permute-start.6 = (f32[4,15,128]{2,1,0:T(8,128)S(1)}, f32[4,15,128]{2,1,0:T(8,128)S(1)}, u32[]{:S(2)}, u32[]{:S(2)}) collective-permute-start(f32[4,15,128]{2,1,0:T(8,128)S(1)} %get-tuple-element.18), channel_id=1, source_target_pairs={{0,8},{4,12},{8,16},{12,20},{16,24},{20,28},{24,32},{28,36},{32,40... | collective-permute-start | bytes 92168 | tf_op jit(solution)/shard_map/ppermute | solution.py:17
  111.6 5.5 %collective-permute-start.5 = (f32[4,15,128]{2,1,0:T(8,128)S(1)}, f32[4,15,128]{2,1,0:T(8,128)S(1)}, u32[]{:S(2)}, u32[]{:S(2)}) collective-permute-start(f32[4,15,128]{2,1,0:T(8,128)S(1)} %get-tuple-element.19), channel_id=1, source_target_pairs={{0,764},{4,0},{8,4},{12,8},{16,12},{20,16},{24,20},{28,24},{32,28}... | collective-permute-start | bytes 92168 | tf_op jit(solution)/shard_map/ppermute | solution.py:17
  117.0 3.1 %collective-permute-start.7 = (f32[4,15,128]{2,1,0:T(8,128)S(1)}, f32[4,15,128]{2,1,0:T(8,128)S(1)}, u32[]{:S(2)}, u32[]{:S(2)}) collective-permute-start(f32[4,15,128]{2,1,0:T(8,128)S(1)} %get-tuple-element.20), channel_id=1, source_target_pairs={{0,760},{4,764},{8,0},{12,4},{16,8},{20,12},{24,16},{28,20},{32,24... | collective-permute-start | bytes 92168 | tf_op jit(solution)/shard_map/ppermute | solution.py:17
  120.2 12.4 %all_gather.14 = f32[32,15,128]{2,0,1:T(8,128)S(1)} all-gather(f32[8,15,128]{2,0,1:T(8,128)} %reduce-scatter.3.cloned.1.call-done), channel_id=1, replica_groups=mesh['dom'=192,'sub'=4] {'sub'}, dimensions={0}, use_global_device_ids=true | all-gather | bytes 307200 | tf_op jit(solution)/shard_map/all_gather | solution.py:93
  132.8 13.3 %all-gather.1 = f32[4,16,15,128]{3,2,1,0:T(8,128)S(1)} all-gather(f32[4,4,15,128]{3,2,1,0:T(8,128)S(1)} %pad_maximum_fusion.2), channel_id=3, replica_groups=mesh['dom'=192,'sub'=4] {'sub'}, dimensions={1}, use_global_device_ids=true | all-gather | bytes 614400 | tf_op jit(solution)/shard_map/all_gather | solution.py:94
  147.1 1.9 gather_fusion.3
  154.7 25.6 %reduce-scatter.5.cloned.1.call-done = f32[8,5,128]{2,0,1:T(8,128)} async-done(((f32[32,5,128]{2,0,1:T(8,128)}), f32[8,5,128]{2,0,1:T(8,128)}) %reduce-scatter.5.cloned.1.call-update) | async-done | bytes 20496 | tf_op jit(solution)/shard_map/reduce_scatter | solution.py:99
  (98 shorter events, 27.4 us)
Async XLA Ops:
  6.5 98.0 %reduce-scatter.3.cloned.1.call-start = ((), (), s32[]{:S(2)}) async-start(), calls=%async_computation.2 | async-start | bytes 307200 | tf_op jit(solution)/shard_map/reduce_scatter | solution.py:99
  7.3 25.9 %copy-start.14 = (s32[1024]{0:T(1024)}, s32[1024]{0:T(1024)S(1)}, u32[]{:S(2)}) copy-start(s32[1024]{0:T(1024)S(1)} %pad_clamp_fusion.2) | copy-start | bytes 12292
  8.7 48.3 %collective-permute-start = (f32[4,5,128]{2,0,1:T(4,128)S(1)}, f32[4,5,128]{2,0,1:T(4,128)S(1)}, u32[]{:S(2)}, u32[]{:S(2)}) collective-permute-start(f32[4,5,128]{2,0,1:T(4,128)S(1)} %get-tuple-element.29), channel_id=1, source_target_pairs={{0,4},{4,8},{8,12},{12,16},{16,20},{20,24},{24,28},{28,32},{32,36}... | collective-permute-start | bytes 30728 | tf_op jit(solution)/shard_map/ppermute | solution.py:17
  10.6 46.4 %collective-permute-start.2 = (f32[4,5,128]{2,0,1:T(4,128)S(1)}, f32[4,5,128]{2,0,1:T(4,128)S(1)}, u32[]{:S(2)}, u32[]{:S(2)}) collective-permute-start(f32[4,5,128]{2,0,1:T(4,128)S(1)} %get-tuple-element.30), channel_id=1, source_target_pairs={{0,8},{4,12},{8,16},{12,20},{16,24},{20,28},{24,32},{28,36},{32,40... | collective-permute-start | bytes 30728 | tf_op jit(solution)/shard_map/ppermute | solution.py:17
  14.9 42.1 %collective-permute-start.1 = (f32[4,5,128]{2,0,1:T(4,128)S(1)}, f32[4,5,128]{2,0,1:T(4,128)S(1)}, u32[]{:S(2)}, u32[]{:S(2)}) collective-permute-start(f32[4,5,128]{2,0,1:T(4,128)S(1)} %get-tuple-element.31), channel_id=1, source_target_pairs={{0,764},{4,0},{8,4},{12,8},{16,12},{20,16},{24,20},{28,24},{32,28}... | collective-permute-start | bytes 30728 | tf_op jit(solution)/shard_map/ppermute | solution.py:17
  26.5 30.5 %collective-permute-start.3 = (f32[4,5,128]{2,0,1:T(4,128)S(1)}, f32[4,5,128]{2,0,1:T(4,128)S(1)}, u32[]{:S(2)}, u32[]{:S(2)}) collective-permute-start(f32[4,5,128]{2,0,1:T(4,128)S(1)} %get-tuple-element.32), channel_id=1, source_target_pairs={{0,760},{4,764},{8,0},{12,4},{16,8},{20,12},{24,16},{28,20},{32,24... | collective-permute-start | bytes 30728 | tf_op jit(solution)/shard_map/ppermute | solution.py:17
  33.2 37.9 %copy-start.15 = (s32[1024]{0:T(1024)}, s32[1024]{0:T(1024)S(1)}, u32[]{:S(2)}) copy-start(s32[1024]{0:T(1024)S(1)} %pad_clamp_fusion.1) | copy-start | bytes 12292
  37.9 6.1 %copy-start = (f32[8,5,128]{2,0,1:T(8,128)S(1)}, f32[8,5,128]{2,0,1:T(8,128)}, u32[]{:S(2)}) copy-start(f32[8,5,128]{2,0,1:T(8,128)} %param.8) | copy-start | bytes 61444
  43.1 13.2 %copy-start.1 = (bf16[32,128,128]{2,1,0:T(8,128)(2,1)}, bf16[32,128,128]{2,1,0:T(8,128)(2,1)S(1)}, u32[]{:S(2)}) copy-start(bf16[32,128,128]{2,1,0:T(8,128)(2,1)S(1)} %get-tuple-element.9) | copy-start | bytes 3145732
  72.8 3.8 %copy-start.3 = (f32[32,5,128]{2,1,0:T(8,128)}, f32[32,5,128]{2,1,0:T(8,128)S(1)}, u32[]{:S(2)}) copy-start(f32[32,5,128]{2,1,0:T(8,128)S(1)} %gather_fusion.1) | copy-start | bytes 245764
  80.5 99.8 %reduce-scatter.5.cloned.1.call-start = ((), (), s32[]{:S(2)}) async-start(), calls=%async_computation.3 | async-start | bytes 102400 | tf_op jit(solution)/shard_map/reduce_scatter | solution.py:99
  106.1 26.7 %collective-permute-start.4 = (f32[4,15,128]{2,1,0:T(8,128)S(1)}, f32[4,15,128]{2,1,0:T(8,128)S(1)}, u32[]{:S(2)}, u32[]{:S(2)}) collective-permute-start(f32[4,15,128]{2,1,0:T(8,128)S(1)} %get-tuple-element.17), channel_id=1, source_target_pairs={{0,4},{4,8},{8,12},{12,16},{16,20},{20,24},{24,28},{28,32},{32,36}... | collective-permute-start | bytes 92168 | tf_op jit(solution)/shard_map/ppermute | solution.py:17
  108.0 24.8 %collective-permute-start.6 = (f32[4,15,128]{2,1,0:T(8,128)S(1)}, f32[4,15,128]{2,1,0:T(8,128)S(1)}, u32[]{:S(2)}, u32[]{:S(2)}) collective-permute-start(f32[4,15,128]{2,1,0:T(8,128)S(1)} %get-tuple-element.18), channel_id=1, source_target_pairs={{0,8},{4,12},{8,16},{12,20},{16,24},{20,28},{24,32},{28,36},{32,40... | collective-permute-start | bytes 92168 | tf_op jit(solution)/shard_map/ppermute | solution.py:17
  111.6 21.2 %collective-permute-start.5 = (f32[4,15,128]{2,1,0:T(8,128)S(1)}, f32[4,15,128]{2,1,0:T(8,128)S(1)}, u32[]{:S(2)}, u32[]{:S(2)}) collective-permute-start(f32[4,15,128]{2,1,0:T(8,128)S(1)} %get-tuple-element.19), channel_id=1, source_target_pairs={{0,764},{4,0},{8,4},{12,8},{16,12},{20,16},{24,20},{28,24},{32,28}... | collective-permute-start | bytes 92168 | tf_op jit(solution)/shard_map/ppermute | solution.py:17
  117.0 15.7 %collective-permute-start.7 = (f32[4,15,128]{2,1,0:T(8,128)S(1)}, f32[4,15,128]{2,1,0:T(8,128)S(1)}, u32[]{:S(2)}, u32[]{:S(2)}) collective-permute-start(f32[4,15,128]{2,1,0:T(8,128)S(1)} %get-tuple-element.20), channel_id=1, source_target_pairs={{0,760},{4,764},{8,0},{12,4},{16,8},{20,12},{24,16},{28,20},{32,24... | collective-permute-start | bytes 92168 | tf_op jit(solution)/shard_map/ppermute | solution.py:17
  147.1 6.0 %copy-start.4 = (f32[32,5,128]{2,1,0:T(8,128)S(1)}, f32[32,5,128]{2,1,0:T(8,128)}, u32[]{:S(2)}) copy-start(f32[32,5,128]{2,1,0:T(8,128)} %copy-done.3) | copy-start | bytes 245764
  149.0 4.2 %copy-start.2 = (bf16[32,128,128]{2,1,0:T(8,128)(2,1)S(1)}, bf16[32,128,128]{2,1,0:T(8,128)(2,1)}, u32[]{:S(2)}) copy-start(bf16[32,128,128]{2,1,0:T(8,128)(2,1)} %copy-done.1) | copy-start | bytes 3145732
  149.0 4.1 %copy-start.7 = (f32[32,5,128]{2,1,0:T(8,128)S(1)}, f32[32,5,128]{2,1,0:T(8,128)}, u32[]{:S(2)}) copy-start(f32[32,5,128]{2,1,0:T(8,128)} %gather_fusion.4) | copy-start | bytes 245764
  149.0 4.2 %copy-start.10 = (f32[32,128]{1,0:T(8,128)S(1)}, f32[32,128]{1,0:T(8,128)}, u32[]{:S(2)}) copy-start(f32[32,128]{1,0:T(8,128)} %convert_reduce_fusion) | copy-start | bytes 49156
  149.0 4.2 %copy-start.11 = (f32[32,128]{1,0:T(8,128)S(1)}, f32[32,128]{1,0:T(8,128)}, u32[]{:S(2)}) copy-start(f32[32,128]{1,0:T(8,128)} %get-tuple-element.27) | copy-start | bytes 49156
  149.0 4.1 %copy-start.12 = (f32[32,128]{1,0:T(8,128)S(1)}, f32[32,128]{1,0:T(8,128)}, u32[]{:S(2)}) copy-start(f32[32,128]{1,0:T(8,128)} %fusion.27) | copy-start | bytes 49156
  149.1 4.7 %copy-start.17 = (s32[32]{0:T(128)S(1)}, s32[32]{0:T(128)}, u32[]{:S(2)}) copy-start(s32[32]{0:T(128)} %param.13) | copy-start | bytes 388
  150.2 4.5 %copy-start.16 = (f32[8,128]{1,0:T(8,128)S(1)}, f32[8,128]{1,0:T(8,128)}, u32[]{:S(2)}) copy-start(f32[8,128]{1,0:T(8,128)} %param.10) | copy-start | bytes 12292
  150.2 30.1 %copy-start.13 = (f32[8,5,128]{2,0,1:T(8,128)S(1)}, f32[8,5,128]{2,0,1:T(8,128)}, u32[]{:S(2)}) copy-start(f32[8,5,128]{2,0,1:T(8,128)} %param.9) | copy-start | bytes 61444
  (4 other events, 7.3 us)
Sparse Core Ops, SparseCore 0:
  80.6 23.8 reduce-scatter.2
  154.8 25.4 reduce-scatter.4
where the time goes:
time: 190 us; the launch traced here: 188 us
  blocking collectives  50 us (26%)
  waiting for transfers between devices  38.6 us (20%)
  starting transfers between devices  36 us (19%)
  local copies, waits for them, and re-layouts  23.8 us (13%)
  other arithmetic  20.3 us (11%)
  between operations  13.9 us (7%)
  matrix products  5.78 us (3%)
    reduce_scatter x2, waiting for transfers between devices, reduce_rows(): return lax.psum_scatter(partial_sum, 'sub', scatter_dimension=0, tiled=True)  38.6 us
    ppermute x8, starting transfers between devices, shifted(): return lax.ppermute(value, axis, pairs)  36 us
    all_gather x2, blocking collectives, share_partition(): lax.all_gather(ghost_packets(values_in), 'sub', axis=1, tiled=True)  25.4 us
    all_gather x2, blocking collectives, share_partition(): lax.all_gather(values_in, 'sub', axis=0, tiled=True)  24.7 us
    unnamed x37, local copies, waits for them, and re-layouts  5.5 us
    reduce_sum x1, other arithmetic, per_device(): jnp.sum(jnp.abs(oriented), axis=1, dtype=jnp.float32).astype(jnp.bfloat16)  5.15 us
  transfers between devices with their start and end apart: 10, of which 2 were waited for; matrix products, arithmetic and copies ran while one was open for 13% of the time, Pallas kernels for 0%

commit v1 on v0

v1 whole, which is shorter than its diff:
```python
import functools

import jax
import jax.numpy as jnp
from jax import lax
from jax.experimental import pallas as pl
from jax.experimental.pallas import tpu as pltpu
from jax.sharding import PartitionSpec as P

MESH = pl.DeviceIdType.MESH
F32, BF16 = jnp.float32, jnp.bfloat16
CURVE_STEPS = (1, -1, 2, -2)
SUBS = 4
OWN = 8
PART = SUBS * OWN
LIST = 4
TILES = 32
CELLS = 128
SLOTS = PART + len(CURVE_STEPS) * SUBS * LIST
ROWS = 8
CHUNKS = 4
NUM_V = 8
NUM_R = 6


def row_sums(owners, parts):
    x = jnp.concatenate(parts, axis=1)
    high = x.astype(BF16)
    rest = x - high.astype(F32)
    mid = rest.astype(BF16)
    low = (rest - mid.astype(F32)).astype(BF16)
    total = jnp.dot(
        owners, jnp.concatenate([high, mid, low], axis=0), preferred_element_type=F32
    )
    return [total[:, i * CELLS : (i + 1) * CELLS] for i in range(len(parts))]


def kernel(
    doms,
    state_h,
    base_h,
    ratio_h,
    send_s,
    row_s,
    col_s,
    flip_s,
    tiles_h,
    out_ref,
    raw,
    weights,
    absolute,
    state,
    base,
    ratio,
    own,
    packets,
    ext,
    gathered,
    terms,
    part_v,
    recv_v,
    mixed,
    own_v,
    packets_v,
    ext_v,
    gathered_v,
    scaled,
    spread,
    fluxes,
    contribution,
    part_r,
    recv_r,
    tile_sem,
    load_sem,
    send_sem,
    recv_sem,
):
    me, sub = lax.axis_index("dom"), lax.axis_index("sub")
    peers = [lax.rem(sub + i, SUBS) for i in range(1, SUBS)]
    targets = [lax.rem(me + (step + doms), doms) for step in CURVE_STEPS]

    barrier = pltpu.get_barrier_semaphore()
    for peer in peers:
        pl.semaphore_signal(barrier, inc=1, device_id=(me, peer), device_id_type=MESH)
    for target in targets:
        for s in range(SUBS):
            pl.semaphore_signal(
                barrier, inc=1, device_id=(target, jnp.int32(s)), device_id_type=MESH
            )

    loads = [
        pltpu.make_async_copy(state_h, state, load_sem.at[0]),
        pltpu.make_async_copy(base_h, base, load_sem.at[1]),
        pltpu.make_async_copy(ratio_h, ratio, load_sem.at[2]),
    ]
    for load in loads:
        load.start()
    per_chunk = TILES // CHUNKS
    tile_loads = [
        pltpu.make_async_copy(
            tiles_h.at[pl.ds(c * per_chunk, per_chunk)],
            raw.at[pl.ds(c * per_chunk, per_chunk)],
            tile_sem.at[c],
        )
        for c in range(CHUNKS)
    ]
    for load in tile_loads:
        load.start()

    def remote(source, target, number, device):
        pltpu.make_async_remote_copy(
            src_ref=source,
            dst_ref=target,
            send_sem=send_sem.at[number],
            recv_sem=recv_sem.at[number],
            device_id=device,
            device_id_type=MESH,
        ).start()

    def drain(sems, number, like):
        pltpu.make_async_copy(like, like, sems.at[number]).wait()

    def share(values, lists, extended, number):
        at = sub * OWN
        for k in range(len(CURVE_STEPS)):
            slot = PART + (k * SUBS + sub) * LIST
            for s in range(SUBS):
                remote(
                    lists.at[pl.ds(k * LIST, LIST)],
                    extended.at[pl.ds(slot, LIST)],
                    number,
                    (targets[k], jnp.int32(s)),
                )
        for peer in peers:
            remote(values, extended.at[pl.ds(at, OWN)], number, (me, peer))
        extended[pl.ds(at, OWN)] = values[...]

    shared = SLOTS - OWN
    flat = lambda ref: ref.reshape(ref.shape[0] * ROWS, CELLS)

    def pick(values, lists):
        for k in range(len(CURVE_STEPS)):
            for j in range(LIST):
                lists[k * LIST + j] = values[jnp.maximum(send_s[0, 0, k, j], 0)]

    loads[0].wait()
    density, energy = state[0], state[4]
    momentum = [state[1 + i] for i in range(3)]
    velocity = [m / density for m in momentum]
    pressure = 0.4 * (
        energy
        - 0.5
        * (momentum[0] * velocity[0] + momentum[1] * velocity[1] + momentum[2] * velocity[2])
    )
    square = velocity[0] * velocity[0] + velocity[1] * velocity[1] + velocity[2] * velocity[2]
    speed = jnp.sqrt(square + 1.4 * pressure / density)
    for i, value in enumerate(
        [density, *velocity, pressure, energy, speed, jnp.zeros_like(speed)]
    ):
        flat(own)[pl.ds(i, OWN, stride=ROWS), :] = value
    pick(own, packets)

    pl.semaphore_wait(barrier, SUBS - 1 + len(CURVE_STEPS) * SUBS)
    share(own, packets, ext, 0)

    lane = lax.broadcasted_iota(jnp.int32, (PART, 3 * TILES), 1)
    lane = lax.rem(lane, TILES)
    tile_rows = jnp.zeros((PART, 3 * TILES), jnp.int32)
    for t in range(TILES):
        tile_rows = jnp.where(lane == t, row_s[t], tile_rows)
    block_row = lax.broadcasted_iota(jnp.int32, (PART, 3 * TILES), 0)
    owners = jnp.where(block_row == tile_rows, 1.0, 0.0).astype(BF16)

    def orient(t, carry):
        flipped = jnp.full((CELLS, CELLS), flip_s[t], jnp.int32) == 1
        total = None
        for d in range(3):
            tile = raw[t, d].astype(F32)
            tile = jnp.where(flipped, -tile, tile.T)
            weights[t, pl.ds(d * CELLS, CELLS), :] = tile.astype(BF16)
            total = jnp.abs(tile) if total is None else total + jnp.abs(tile)
        absolute[t] = total.astype(BF16)
        return carry

    for c in range(CHUNKS):
        tile_loads[c].wait()
        lax.fori_loop(c * per_chunk, (c + 1) * per_chunk, orient, 0)
    ones = jnp.ones((TILES, CELLS), F32)
    scaled[pl.ds(5 * TILES, TILES), :] = ones
    for v in (6, 7):
        scaled[pl.ds(v * TILES, TILES), :] = jnp.zeros_like(ones)
    for d in range(3):
        for v in (5, 6, 7):
            fluxes[pl.ds((d * ROWS + v) * TILES, TILES), :] = jnp.zeros_like(ones)

    drain(recv_sem, 0, ext.at[pl.ds(0, shared)])

    def slope(t, carry):
        at = pl.multiple_of(t * ROWS, ROWS)
        column = ext[col_s[t]]
        gathered[pl.ds(at, ROWS), :] = column
        column = column.astype(BF16)
        for d in range(3):
            terms[pl.ds(pl.multiple_of((t * 3 + d) * ROWS, ROWS), ROWS), :] = jnp.dot(
                column, weights[t, pl.ds(d * CELLS, CELLS), :], preferred_element_type=F32
            )
        return carry

    lax.fori_loop(0, TILES, slope, 0, unroll=4)

    def term(d, v):
        return terms[pl.ds(d * ROWS + v, TILES, stride=3 * ROWS), :]

    shear = [[term(d, 1 + i) for i in range(3)] for d in range(3)]
    third = (2.0 / 3.0) * (shear[0][0] + shear[1][1] + shear[2][2])
    sums = row_sums(
        owners,
        [
            2.0 * shear[0][0] - third,
            2.0 * shear[1][1] - third,
            shear[0][1] + shear[1][0],
            shear[0][2] + shear[2][0],
            shear[1][2] + shear[2][1],
        ]
        + [term(d, 4) for d in range(3)]
        + [term(d, 0) for d in range(3)],
    )
    rho, v0, v1, v2, press = [flat(ext)[pl.ds(v, PART, stride=ROWS), :] for v in range(5)]
    s00, s11, s01, s02, s12 = [0.3 * s for s in sums[:5]]
    s22 = -(s00 + s11)
    level = press / rho
    heat = [1.46 * (sums[5 + d] - level * sums[8 + d]) / rho for d in range(3)]
    work = [
        s00 * v0 + s01 * v1 + s02 * v2 + heat[0],
        s01 * v0 + s11 * v1 + s12 * v2 + heat[1],
        s02 * v0 + s12 * v1 + s22 * v2 + heat[2],
    ]
    for c, value in enumerate([s00, s11, s01, s02, s12, *work]):
        for s in range(SUBS):
            part_v[pl.ds((s * NUM_V + c) * OWN, OWN), :] = value[s * OWN : (s + 1) * OWN]

    def reduce_to_owners(part, recv, count, number):
        size = count * OWN
        for i, peer in enumerate(peers):
            remote(
                part.at[pl.ds(pl.multiple_of(peer * size, size), size)],
                recv.at[pl.ds(i * size, size)],
                number,
                (me, peer),
            )

    def reduced(part, recv, count, number):
        size = count * OWN
        drain(recv_sem, number, recv)
        total = part[pl.ds(pl.multiple_of(sub * size, size), size), :]
        for i in range(SUBS - 1):
            total = total + recv[pl.ds(i * size, size), :]
        return total

    reduce_to_owners(part_v, recv_v, NUM_V, 1)

    rho, v0, v1, v2, press, ener, wave = [
        gathered[pl.ds(v, TILES, stride=ROWS), :] for v in range(7)
    ]
    vel = [v0, v1, v2]
    mom = [rho * v for v in vel]
    for v, value in enumerate([rho, *mom, ener]):
        scaled[pl.ds(v * TILES, TILES), :] = wave * value

    def dissipate(t, carry):
        left = scaled[pl.ds(t, ROWS, stride=TILES), :].astype(BF16)
        spread[pl.ds(pl.multiple_of(t * ROWS, ROWS), ROWS), :] = jnp.dot(
            left, absolute[t], preferred_element_type=F32
        )
        return carry

    lax.fori_loop(0, TILES, dissipate, 0, unroll=4)

    mixed[...] = reduced(part_v, recv_v, NUM_V, 1)
    for r in range(OWN):
        own_v[r] = mixed[pl.ds(r, ROWS, stride=OWN), :]
    pick(own_v, packets_v)
    share(own_v, packets_v, ext_v, 2)
    drain(recv_sem, 2, ext_v.at[pl.ds(0, shared)])

    def gather_v(t, carry):
        gathered_v[pl.ds(pl.multiple_of(t * ROWS, ROWS), ROWS), :] = ext_v[col_s[t]]
        return carry

    lax.fori_loop(0, TILES, gather_v, 0, unroll=8)
    s00, s11, s01, s02, s12, w0, w1, w2 = [
        gathered_v[pl.ds(c, TILES, stride=ROWS), :] for c in range(NUM_V)
    ]
    stress = [[s00, s01, s02], [s01, s11, s12], [s02, s12, -(s00 + s11)]]
    work = [w0, w1, w2]
    for d in range(3):
        values = [mom[d]]
        for i in range(3):
            flow = mom[i] * vel[d]
            if i == d:
                flow = flow + press
            values.append(flow - stress[d][i])
        values.append((ener + press) * vel[d] - work[d])
        for v, value in enumerate(values):
            fluxes[pl.ds((d * ROWS + v) * TILES, TILES), :] = value

    def flux(t, carry):
        at = pl.multiple_of(t * ROWS, ROWS)
        left = jnp.concatenate(
            [fluxes[pl.ds(d * ROWS * TILES + t, ROWS, stride=TILES), :] for d in range(3)],
            axis=1,
        ).astype(BF16)
        total = jnp.dot(left, weights[t], preferred_element_type=F32)
        contribution[pl.ds(at, ROWS), :] = total - 0.1 * spread[pl.ds(at, ROWS), :]
        return carry

    lax.fori_loop(0, TILES, flux, 0, unroll=4)

    sums = row_sums(
        owners, [contribution[pl.ds(v, TILES, stride=ROWS), :] for v in range(NUM_R)]
    )
    for c, value in enumerate(sums):
        for s in range(SUBS):
            part_r[pl.ds((s * NUM_R + c) * OWN, OWN), :] = value[s * OWN : (s + 1) * OWN]
    reduce_to_owners(part_r, recv_r, NUM_R, 3)

    loads[1].wait()
    loads[2].wait()
    total = reduced(part_r, recv_r, NUM_R, 3)
    absolute_sum = total[5 * OWN : 6 * OWN] * speed
    half = 0.5 * ratio[...]
    for v, value in enumerate([density, *momentum, energy]):
        residual = total[v * OWN : (v + 1) * OWN] - absolute_sum * value
        out_ref[v] = base[v] - half * residual

    drain(send_sem, 0, ext.at[pl.ds(0, shared)])
    drain(send_sem, 1, recv_v)
    drain(send_sem, 2, ext_v.at[pl.ds(0, shared)])
    drain(send_sem, 3, recv_r)


def per_device(
    section_state, base_state, ratio, send_list, face_tiles, tile_row, tile_col, tile_flip
):
    any_space = pl.BlockSpec(memory_space=pl.ANY)
    smem = pl.BlockSpec(memory_space=pltpu.SMEM)
    blocks = lambda count: pltpu.VMEM((count, ROWS, CELLS), F32)
    row = lambda count: pltpu.VMEM((count, CELLS), F32)
    updated = pl.pallas_call(
        functools.partial(kernel, lax.axis_size("dom")),
        out_shape=jax.ShapeDtypeStruct((5, OWN, CELLS), F32),
        in_specs=[any_space] * 3 + [smem] * 4 + [any_space],
        out_specs=pl.BlockSpec(memory_space=pltpu.VMEM),
        scratch_shapes=[
            pltpu.VMEM((TILES, 3, CELLS, CELLS), BF16),
            pltpu.VMEM((TILES, 3 * CELLS, CELLS), BF16),
            pltpu.VMEM((TILES, CELLS, CELLS), BF16),
            pltpu.VMEM((5, OWN, CELLS), F32),
            pltpu.VMEM((5, OWN, CELLS), F32),
            pltpu.VMEM((OWN, CELLS), F32),
            blocks(OWN),
            blocks(len(CURVE_STEPS) * LIST),
            blocks(SLOTS),
            row(TILES * ROWS),
            row(TILES * 3 * ROWS),
            row(SUBS * NUM_V * OWN),
            row((SUBS - 1) * NUM_V * OWN),
            row(NUM_V * OWN),
            blocks(OWN),
            blocks(len(CURVE_STEPS) * LIST),
            blocks(SLOTS),
            row(TILES * ROWS),
            row(ROWS * TILES),
            row(TILES * ROWS),
            row(3 * ROWS * TILES),
            row(TILES * ROWS),
            row(SUBS * NUM_R * OWN),
            row((SUBS - 1) * NUM_R * OWN),
            pltpu.SemaphoreType.DMA((CHUNKS,)),
            pltpu.SemaphoreType.DMA((3,)),
            pltpu.SemaphoreType.DMA((4,)),
            pltpu.SemaphoreType.DMA((4,)),
        ],
        compiler_params=pltpu.CompilerParams(
            collective_id=0, has_side_effects=True, vmem_limit_bytes=60 * 1024 * 1024
        ),
    )(
        jnp.transpose(section_state, (1, 0, 2)),
        jnp.transpose(base_state, (1, 0, 2)),
        ratio,
        send_list,
        tile_row,
        tile_col,
        tile_flip,
        face_tiles,
    )
    return jnp.transpose(updated, (1, 0, 2))


def solution(mesh):
    return jax.shard_map(
        per_device,
        mesh=mesh,
        in_specs=(
            P(("dom", "sub"), None, None),
            P(("dom", "sub"), None, None),
            P(("dom", "sub"), None),
            P("dom", "sub", None, None),
            P(("dom", "sub"), None, None, None),
            P(("dom", "sub")),
            P(("dom", "sub")),
            P(("dom", "sub")),
        ),
        out_specs=P(("dom", "sub"), None, None),
        check_vma=False,
    )
```

time: 190 us -> 45.7 us (0.24)
  the two profiles are of different devices: /device:TPU:8 before, /device:TPU:2 now
where the time goes in v1:
time: 45.7 us; the launch traced here: 45.5 us
  Pallas kernels  44.1 us (96%)
  local copies, waits for them, and re-layouts  1.34 us (3%)
    pallas_call x1, Pallas kernels, per_device(): pl.pallas_call(functools.partial(kernel, lax.axis_size('dom')), out_shape...  44.1 us
    unnamed x1, local copies, waits for them, and re-layouts  1.34 us

profile of v1, /device:TPU:2, one launch (start us, length us, event | category | flops | bytes accessed | tf_op | source)
XLA Modules:
  0.0 45.5 jit_solution(13863950979606604876)
XLA Ops:
  0.0 44.1 %shard_map.82 = f32[5,8,128]{2,1,0:T(8,128)} custom-call(f32[5,8,128]{2,1,0:T(8,128)} %bitcast.4, f32[5,8,128]{2,1,0:T(8,128)} %bitcast.5, f32[8,128]{1,0:T(8,128)} %ratio_h.1, s32[1,1,4,4]{3,2,1,0:T(4,128)} %send_s.1, s32[32]{0:T(128)} %row_s.1, s32[32]{0:T(128)} %col_s.1, s32[32]{0:T(128)} %flip_s.1, bf16[32,3,128,128]{3,2,1,0:T(8,128)(2,1)} %tiles_h.1), custom_call_target="tpu_custom_call" | custom-call | tf_op jit(solution)/shard_map/pallas_call | solution.py:349
  44.1 1.3 %copy.10 = f32[8,5,128]{2,0,1:T(8,128)} copy(f32[8,5,128]{2,0,1:T(8,128)} %bitcast.3) | data formatting | bytes 40960

commit v2 on v1

--- a/solution.py
+++ b/solution.py
@@ -40,10 +40,10 @@
     state_h,
     base_h,
     ratio_h,
-    send_s,
-    row_s,
-    col_s,
-    flip_s,
+    send_h,
+    row_h,
+    col_h,
+    flip_h,
     tiles_h,
     out_ref,
     raw,
@@ -70,6 +70,10 @@
     contribution,
     part_r,
     recv_r,
+    send_s,
+    row_s,
+    col_s,
+    flip_s,
     tile_sem,
     load_sem,
     send_sem,
@@ -77,21 +81,32 @@
 ):
     me, sub = lax.axis_index("dom"), lax.axis_index("sub")
     peers = [lax.rem(sub + i, SUBS) for i in range(1, SUBS)]
-    targets = [lax.rem(me + (step + doms), doms) for step in CURVE_STEPS]
+    targets = [me + step for step in CURVE_STEPS]
+    inside = lambda dom: (dom >= 0) & (dom < doms)
 
     barrier = pltpu.get_barrier_semaphore()
     for peer in peers:
         pl.semaphore_signal(barrier, inc=1, device_id=(me, peer), device_id_type=MESH)
+    greeted = SUBS - 1
     for target in targets:
-        for s in range(SUBS):
-            pl.semaphore_signal(
-                barrier, inc=1, device_id=(target, jnp.int32(s)), device_id_type=MESH
-            )
+        greeted = greeted + jnp.where(inside(target), SUBS, 0)
+
+        @pl.when(inside(target))
+        def _():
+            for s in range(SUBS):
+                pl.semaphore_signal(
+                    barrier, inc=1, device_id=(target, jnp.int32(s)), device_id_type=MESH
+                )
+
 
     loads = [
         pltpu.make_async_copy(state_h, state, load_sem.at[0]),
         pltpu.make_async_copy(base_h, base, load_sem.at[1]),
         pltpu.make_async_copy(ratio_h, ratio, load_sem.at[2]),
+        pltpu.make_async_copy(send_h, send_s, load_sem.at[3]),
+        pltpu.make_async_copy(row_h, row_s, load_sem.at[4]),
+        pltpu.make_async_copy(col_h, col_s, load_sem.at[5]),
+        pltpu.make_async_copy(flip_h, flip_s, load_sem.at[6]),
     ]
     for load in loads:
         load.start()
@@ -120,22 +135,39 @@
     def drain(sems, number, like):
         pltpu.make_async_copy(like, like, sems.at[number]).wait()
 
-    def share(values, lists, extended, number):
+    def share(values, lists, extended, rows, first):
         at = sub * OWN
-        for k in range(len(CURVE_STEPS)):
+        for k in (2, 3, 1, 0):
             slot = PART + (k * SUBS + sub) * LIST
-            for s in range(SUBS):
-                remote(
-                    lists.at[pl.ds(k * LIST, LIST)],
-                    extended.at[pl.ds(slot, LIST)],
-                    number,
-                    (targets[k], jnp.int32(s)),
-                )
+
+            @pl.when(inside(targets[k]))
+            def _():
+                for i in (2, 1, 3, 0):
+                    remote(
+                        lists.at[pl.ds(k * LIST, LIST), pl.ds(0, rows)],
+                        extended.at[pl.ds(slot, LIST), pl.ds(0, rows)],
+                        first + k,
+                        (targets[k], lax.rem(sub + i, SUBS)),
+                    )
+
         for peer in peers:
-            remote(values, extended.at[pl.ds(at, OWN)], number, (me, peer))
+            remote(
+                values.at[:, pl.ds(0, rows)],
+                extended.at[pl.ds(at, OWN), pl.ds(0, rows)],
+                first + 4,
+                (me, peer),
+            )
         extended[pl.ds(at, OWN)] = values[...]
 
-    shared = SLOTS - OWN
+    def shared(sems, extended, rows, first, sign):
+        for k, step in enumerate(CURVE_STEPS):
+
+            @pl.when(inside(me + sign * step))
+            def _():
+                drain(sems, first + k, extended.at[pl.ds(0, SUBS * LIST), pl.ds(0, rows)])
+
+        drain(sems, first + 4, extended.at[pl.ds(0, PART - OWN), pl.ds(0, rows)])
+
     flat = lambda ref: ref.reshape(ref.shape[0] * ROWS, CELLS)
 
     def pick(values, lists):
@@ -144,6 +176,7 @@
                 lists[k * LIST + j] = values[jnp.maximum(send_s[0, 0, k, j], 0)]
 
     loads[0].wait()
+    loads[3].wait()
     density, energy = state[0], state[4]
     momentum = [state[1 + i] for i in range(3)]
     velocity = [m / density for m in momentum]
@@ -155,14 +188,16 @@
     square = velocity[0] * velocity[0] + velocity[1] * velocity[1] + velocity[2] * velocity[2]
     speed = jnp.sqrt(square + 1.4 * pressure / density)
     for i, value in enumerate(
-        [density, *velocity, pressure, energy, speed, jnp.zeros_like(speed)]
+        [density, *velocity, pressure]
     ):
         flat(own)[pl.ds(i, OWN, stride=ROWS), :] = value
     pick(own, packets)
 
-    pl.semaphore_wait(barrier, SUBS - 1 + len(CURVE_STEPS) * SUBS)
-    share(own, packets, ext, 0)
-
+    pl.semaphore_wait(barrier, greeted)
+    share(own, packets, ext, 5, 0)
+
+    for load in loads[4:]:
+        load.wait()
     lane = lax.broadcasted_iota(jnp.int32, (PART, 3 * TILES), 1)
     lane = lax.rem(lane, TILES)
     tile_rows = jnp.zeros((PART, 3 * TILES), jnp.int32)
@@ -193,7 +228,7 @@
         for v in (5, 6, 7):
             fluxes[pl.ds((d * ROWS + v) * TILES, TILES), :] = jnp.zeros_like(ones)
 
-    drain(recv_sem, 0, ext.at[pl.ds(0, shared)])
+    shared(recv_sem, ext, 5, 0, -1)
 
     def slope(t, carry):
         at = pl.multiple_of(t * ROWS, ROWS)
@@ -206,7 +241,7 @@
             )
         return carry
 
-    lax.fori_loop(0, TILES, slope, 0, unroll=4)
+    lax.fori_loop(0, TILES, slope, 0, unroll=TILES)
 
     def term(d, v):
         return terms[pl.ds(d * ROWS + v, TILES, stride=3 * ROWS), :]
@@ -257,12 +292,13 @@
             total = total + recv[pl.ds(i * size, size), :]
         return total
 
-    reduce_to_owners(part_v, recv_v, NUM_V, 1)
-
-    rho, v0, v1, v2, press, ener, wave = [
-        gathered[pl.ds(v, TILES, stride=ROWS), :] for v in range(7)
-    ]
+    reduce_to_owners(part_v, recv_v, NUM_V, 10)
+
+    rho, v0, v1, v2, press = [gathered[pl.ds(v, TILES, stride=ROWS), :] for v in range(5)]
     vel = [v0, v1, v2]
+    square = v0 * v0 + v1 * v1 + v2 * v2
+    ener = 2.5 * press + 0.5 * rho * square
+    wave = jnp.sqrt(square + 1.4 * press / rho)
     mom = [rho * v for v in vel]
     for v, value in enumerate([rho, *mom, ener]):
         scaled[pl.ds(v * TILES, TILES), :] = wave * value
@@ -274,20 +310,20 @@
         )
         return carry
 
-    lax.fori_loop(0, TILES, dissipate, 0, unroll=4)
-
-    mixed[...] = reduced(part_v, recv_v, NUM_V, 1)
+    lax.fori_loop(0, TILES, dissipate, 0, unroll=TILES)
+
+    mixed[...] = reduced(part_v, recv_v, NUM_V, 10)
     for r in range(OWN):
         own_v[r] = mixed[pl.ds(r, ROWS, stride=OWN), :]
     pick(own_v, packets_v)
-    share(own_v, packets_v, ext_v, 2)
-    drain(recv_sem, 2, ext_v.at[pl.ds(0, shared)])
+    share(own_v, packets_v, ext_v, ROWS, 5)
+    shared(recv_sem, ext_v, ROWS, 5, -1)
 
     def gather_v(t, carry):
         gathered_v[pl.ds(pl.multiple_of(t * ROWS, ROWS), ROWS), :] = ext_v[col_s[t]]
         return carry
 
-    lax.fori_loop(0, TILES, gather_v, 0, unroll=8)
+    lax.fori_loop(0, TILES, gather_v, 0, unroll=TILES)
     s00, s11, s01, s02, s12, w0, w1, w2 = [
         gathered_v[pl.ds(c, TILES, stride=ROWS), :] for c in range(NUM_V)
     ]
@@ -314,7 +350,7 @@
         contribution[pl.ds(at, ROWS), :] = total - 0.1 * spread[pl.ds(at, ROWS), :]
         return carry
 
-    lax.fori_loop(0, TILES, flux, 0, unroll=4)
+    lax.fori_loop(0, TILES, flux, 0, unroll=TILES)
 
     sums = row_sums(
         owners, [contribution[pl.ds(v, TILES, stride=ROWS), :] for v in range(NUM_R)]
@@ -322,34 +358,34 @@
     for c, value in enumerate(sums):
         for s in range(SUBS):
             part_r[pl.ds((s * NUM_R + c) * OWN, OWN), :] = value[s * OWN : (s + 1) * OWN]
-    reduce_to_owners(part_r, recv_r, NUM_R, 3)
+    reduce_to_owners(part_r, recv_r, NUM_R, 11)
 
     loads[1].wait()
     loads[2].wait()
-    total = reduced(part_r, recv_r, NUM_R, 3)
+    total = reduced(part_r, recv_r, NUM_R, 11)
     absolute_sum = total[5 * OWN : 6 * OWN] * speed
     half = 0.5 * ratio[...]
     for v, value in enumerate([density, *momentum, energy]):
         residual = total[v * OWN : (v + 1) * OWN] - absolute_sum * value
         out_ref[v] = base[v] - half * residual
 
-    drain(send_sem, 0, ext.at[pl.ds(0, shared)])
-    drain(send_sem, 1, recv_v)
-    drain(send_sem, 2, ext_v.at[pl.ds(0, shared)])
-    drain(send_sem, 3, recv_r)
+    shared(send_sem, ext, 5, 0, 1)
+    drain(send_sem, 10, recv_v)
+    shared(send_sem, ext_v, ROWS, 5, 1)
+    drain(send_sem, 11, recv_r)
 
 
 def per_device(
     section_state, base_state, ratio, send_list, face_tiles, tile_row, tile_col, tile_flip
 ):
     any_space = pl.BlockSpec(memory_space=pl.ANY)
-    smem = pl.BlockSpec(memory_space=pltpu.SMEM)
+    scalars = lambda *shape: pltpu.SMEM(shape, jnp.int32)
     blocks = lambda count: pltpu.VMEM((count, ROWS, CELLS), F32)
     row = lambda count: pltpu.VMEM((count, CELLS), F32)
     updated = pl.pallas_call(
         functools.partial(kernel, lax.axis_size("dom")),
         out_shape=jax.ShapeDtypeStruct((5, OWN, CELLS), F32),
-        in_specs=[any_space] * 3 + [smem] * 4 + [any_space],
+        in_specs=[any_space] * 8,
         out_specs=pl.BlockSpec(memory_space=pltpu.VMEM),
         scratch_shapes=[
             pltpu.VMEM((TILES, 3, CELLS, CELLS), BF16),
@@ -376,10 +412,14 @@
             row(TILES * ROWS),
             row(SUBS * NUM_R * OWN),
             row((SUBS - 1) * NUM_R * OWN),
+            scalars(*send_list.shape),
+            scalars(TILES),
+            scalars(TILES),
+            scalars(TILES),
             pltpu.SemaphoreType.DMA((CHUNKS,)),
-            pltpu.SemaphoreType.DMA((3,)),
-            pltpu.SemaphoreType.DMA((4,)),
-            pltpu.SemaphoreType.DMA((4,)),
+            pltpu.SemaphoreType.DMA((7,)),
+            pltpu.SemaphoreType.DMA((12,)),
+            pltpu.SemaphoreType.DMA((12,)),
         ],
         compiler_params=pltpu.CompilerParams(
             collective_id=0, has_side_effects=True, vmem_limit_bytes=60 * 1024 * 1024

time: 45.7 us -> 40.1 us (0.88)
  the two profiles are of different devices: /device:TPU:2 before, /device:TPU:32 now
where the time goes in v2:
time: 40.1 us; the launch traced here: 39.9 us
  Pallas kernels  38.6 us (96%)
  local copies, waits for them, and re-layouts  1.34 us (3%)
    pallas_call x1, Pallas kernels, per_device(): pl.pallas_call(functools.partial(kernel, lax.axis_size('dom')), out_shape...  38.6 us
    unnamed x1, local copies, waits for them, and re-layouts  1.34 us

profile of v2, /device:TPU:32, one launch (start us, length us, event | category | flops | bytes accessed | tf_op | source)
XLA Modules:
  0.0 39.9 jit_solution(16937992220913864951)
XLA Ops:
  0.0 38.6 %shard_map.82 = f32[5,8,128]{2,1,0:T(8,128)} custom-call(f32[5,8,128]{2,1,0:T(8,128)} %bitcast.4, f32[5,8,128]{2,1,0:T(8,128)} %bitcast.5, f32[8,128]{1,0:T(8,128)} %ratio_h.1, s32[1,1,4,4]{3,2,1,0:T(4,128)} %send_h.1, s32[32]{0:T(128)} %row_h.1, s32[32]{0:T(128)} %col_h.1, s32[32]{0:T(128)} %flip_h.1, bf16[32,3,128,128]{3,2,1,0:T(8,128)(2,1)} %tiles_h.1), custom_call_target="tpu_custom_call" | custom-call | tf_op jit(solution)/shard_map/pallas_call | solution.py:385
  38.6 1.3 %copy.10 = f32[8,5,128]{2,0,1:T(8,128)} copy(f32[8,5,128]{2,0,1:T(8,128)} %bitcast.3) | data formatting | bytes 40960

commit v3 on v2

--- a/solution.py
+++ b/solution.py
@@ -80,13 +80,11 @@
     recv_sem,
 ):
     me, sub = lax.axis_index("dom"), lax.axis_index("sub")
-    peers = [lax.rem(sub + i, SUBS) for i in range(1, SUBS)]
+    peers = [lax.rem(sub + i, SUBS) for i in (2, 1, 3)]
     targets = [me + step for step in CURVE_STEPS]
     inside = lambda dom: (dom >= 0) & (dom < doms)
 
     barrier = pltpu.get_barrier_semaphore()
-    for peer in peers:
-        pl.semaphore_signal(barrier, inc=1, device_id=(me, peer), device_id_type=MESH)
     greeted = SUBS - 1
     for target in targets:
         greeted = greeted + jnp.where(inside(target), SUBS, 0)
@@ -98,6 +96,8 @@
                     barrier, inc=1, device_id=(target, jnp.int32(s)), device_id_type=MESH
                 )
 
+    for peer in peers:
+        pl.semaphore_signal(barrier, inc=1, device_id=(me, peer), device_id_type=MESH)
 
     loads = [
         pltpu.make_async_copy(state_h, state, load_sem.at[0]),
@@ -142,6 +142,8 @@
 
             @pl.when(inside(targets[k]))
             def _():
+                for j in range(LIST):
+                    lists[k * LIST + j] = values[jnp.maximum(send_s[0, 0, k, j], 0)]
                 for i in (2, 1, 3, 0):
                     remote(
                         lists.at[pl.ds(k * LIST, LIST), pl.ds(0, rows)],
@@ -169,11 +171,6 @@
         drain(sems, first + 4, extended.at[pl.ds(0, PART - OWN), pl.ds(0, rows)])
 
     flat = lambda ref: ref.reshape(ref.shape[0] * ROWS, CELLS)
-
-    def pick(values, lists):
-        for k in range(len(CURVE_STEPS)):
-            for j in range(LIST):
-                lists[k * LIST + j] = values[jnp.maximum(send_s[0, 0, k, j], 0)]
 
     loads[0].wait()
     loads[3].wait()
@@ -191,7 +188,6 @@
         [density, *velocity, pressure]
     ):
         flat(own)[pl.ds(i, OWN, stride=ROWS), :] = value
-    pick(own, packets)
 
     pl.semaphore_wait(barrier, greeted)
     share(own, packets, ext, 5, 0)
@@ -212,7 +208,7 @@
         for d in range(3):
             tile = raw[t, d].astype(F32)
             tile = jnp.where(flipped, -tile, tile.T)
-            weights[t, pl.ds(d * CELLS, CELLS), :] = tile.astype(BF16)
+            weights[t, :, pl.ds(d * CELLS, CELLS)] = tile.astype(BF16)
             total = jnp.abs(tile) if total is None else total + jnp.abs(tile)
         absolute[t] = total.astype(BF16)
         return carry
@@ -230,18 +226,23 @@
 
     shared(recv_sem, ext, 5, 0, -1)
 
-    def slope(t, carry):
-        at = pl.multiple_of(t * ROWS, ROWS)
-        column = ext[col_s[t]]
-        gathered[pl.ds(at, ROWS), :] = column
-        column = column.astype(BF16)
-        for d in range(3):
-            terms[pl.ds(pl.multiple_of((t * 3 + d) * ROWS, ROWS), ROWS), :] = jnp.dot(
-                column, weights[t, pl.ds(d * CELLS, CELLS), :], preferred_element_type=F32
-            )
+    def slope(u, carry):
+        zero = jnp.zeros((ROWS, CELLS), BF16)
+        cols = []
+        for i in range(2):
+            column = ext[col_s[2 * u + i]]
+            gathered[pl.ds(pl.multiple_of((2 * u + i) * ROWS, ROWS), ROWS), :] = column
+            cols.append(column.astype(BF16))
+        left = jnp.concatenate([jnp.concatenate([cols[0], zero], axis=1), jnp.concatenate([zero, cols[1]], axis=1)], axis=0)
+        out = jnp.dot(left, jnp.concatenate([weights[2 * u], weights[2 * u + 1]], axis=0), preferred_element_type=F32)
+        for i in range(2):
+          for d in range(3):
+            terms[pl.ds(pl.multiple_of(((2 * u + i) * 3 + d) * ROWS, ROWS), ROWS), :] = out[
+                i * ROWS : (i + 1) * ROWS, d * CELLS : (d + 1) * CELLS
+            ]
         return carry
 
-    lax.fori_loop(0, TILES, slope, 0, unroll=TILES)
+    lax.fori_loop(0, TILES // 2, slope, 0, unroll=TILES // 2)
 
     def term(d, v):
         return terms[pl.ds(d * ROWS + v, TILES, stride=3 * ROWS), :]
@@ -315,7 +316,6 @@
     mixed[...] = reduced(part_v, recv_v, NUM_V, 10)
     for r in range(OWN):
         own_v[r] = mixed[pl.ds(r, ROWS, stride=OWN), :]
-    pick(own_v, packets_v)
     share(own_v, packets_v, ext_v, ROWS, 5)
     shared(recv_sem, ext_v, ROWS, 5, -1)
 
@@ -346,7 +346,11 @@
             [fluxes[pl.ds(d * ROWS * TILES + t, ROWS, stride=TILES), :] for d in range(3)],
             axis=1,
         ).astype(BF16)
-        total = jnp.dot(left, weights[t], preferred_element_type=F32)
+        total = jnp.dot(
+            left,
+            jnp.concatenate([weights[t, :, pl.ds(d * CELLS, CELLS)] for d in range(3)], axis=0),
+            preferred_element_type=F32,
+        )
         contribution[pl.ds(at, ROWS), :] = total - 0.1 * spread[pl.ds(at, ROWS), :]
         return carry
 
@@ -389,7 +393,7 @@
         out_specs=pl.BlockSpec(memory_space=pltpu.VMEM),
         scratch_shapes=[
             pltpu.VMEM((TILES, 3, CELLS, CELLS), BF16),
-            pltpu.VMEM((TILES, 3 * CELLS, CELLS), BF16),
+            pltpu.VMEM((TILES, CELLS, 3 * CELLS), BF16),
             pltpu.VMEM((TILES, CELLS, CELLS), BF16),
             pltpu.VMEM((5, OWN, CELLS), F32),
             pltpu.VMEM((5, OWN, CELLS), F32),

time: 40.1 us -> 39.6 us (0.988)
  Pallas kernels: 38.6 us -> 38.1 us
    pallas_call x1, Pallas kernels: 38.6 us -> 38.1 us  [per_device(): pl.pallas_call(functools.partial(kernel, lax.axis_size('dom')), out_shape...]
where the time goes in v3:
time: 39.6 us; the launch traced here: 39.5 us
  Pallas kernels  38.1 us (96%)
  local copies, waits for them, and re-layouts  1.34 us (3%)
    pallas_call x1, Pallas kernels, per_device(): pl.pallas_call(functools.partial(kernel, lax.axis_size('dom')), out_shape...  38.1 us
    unnamed x1, local copies, waits for them, and re-layouts  1.34 us

profile of v3, /device:TPU:32, one launch (start us, length us, event | category | flops | bytes accessed | tf_op | source)
XLA Modules:
  0.0 39.5 jit_solution(8223983218530168341)
XLA Ops:
  0.0 38.1 %shard_map.82 = f32[5,8,128]{2,1,0:T(8,128)} custom-call(f32[5,8,128]{2,1,0:T(8,128)} %bitcast.4, f32[5,8,128]{2,1,0:T(8,128)} %bitcast.5, f32[8,128]{1,0:T(8,128)} %ratio_h.1, s32[1,1,4,4]{3,2,1,0:T(4,128)} %send_h.1, s32[32]{0:T(128)} %row_h.1, s32[32]{0:T(128)} %col_h.1, s32[32]{0:T(128)} %flip_h.1, bf16[32,3,128,128]{3,2,1,0:T(8,128)(2,1)} %tiles_h.1), custom_call_target="tpu_custom_call" | custom-call | tf_op jit(solution)/shard_map/pallas_call | solution.py:389
  38.1 1.3 %copy.10 = f32[8,5,128]{2,0,1:T(8,128)} copy(f32[8,5,128]{2,0,1:T(8,128)} %bitcast.3) | data formatting | bytes 40960

commit v4 on v3

--- a/solution.py
+++ b/solution.py
@@ -64,6 +64,10 @@
     packets_v,
     ext_v,
     gathered_v,
+    own_w,
+    packets_w,
+    ext_w,
+    gathered_w,
     scaled,
     spread,
     fluxes,
@@ -137,28 +141,42 @@
 
     def share(values, lists, extended, rows, first):
         at = sub * OWN
-        for k in (2, 3, 1, 0):
-            slot = PART + (k * SUBS + sub) * LIST
-
-            @pl.when(inside(targets[k]))
-            def _():
-                for j in range(LIST):
-                    lists[k * LIST + j] = values[jnp.maximum(send_s[0, 0, k, j], 0)]
-                for i in (2, 1, 3, 0):
-                    remote(
-                        lists.at[pl.ds(k * LIST, LIST), pl.ds(0, rows)],
-                        extended.at[pl.ds(slot, LIST), pl.ds(0, rows)],
-                        first + k,
-                        (targets[k], lax.rem(sub + i, SUBS)),
-                    )
-
-        for peer in peers:
+        def pick(k):
+            for j in range(LIST):
+                lists[k * LIST + j] = values[jnp.maximum(send_s[0, 0, k, j], 0)]
+
+        def send(k, i):
             remote(
-                values.at[:, pl.ds(0, rows)],
-                extended.at[pl.ds(at, OWN), pl.ds(0, rows)],
-                first + 4,
-                (me, peer),
+                lists.at[pl.ds(k * LIST, LIST), pl.ds(0, rows)],
+                extended.at[pl.ds(PART + (k * SUBS + sub) * LIST, LIST), pl.ds(0, rows)],
+                first + k,
+                (targets[k], lax.rem(sub + i, SUBS)),
             )
+
+        def send_own(which):
+            for peer in which:
+                remote(
+                    values.at[:, pl.ds(0, rows)],
+                    extended.at[pl.ds(at, OWN), pl.ds(0, rows)],
+                    first + 4,
+                    (me, peer),
+                )
+
+        for turn in range(2):
+            for k in (0, 1):
+                @pl.when(inside(targets[k]) & (lax.rem(me + k + turn, 2) == 1))
+                def _():
+                    pick(k)
+                    for i in (2, 1, 3, 0):
+                        send(k, i)
+            if turn == 0:
+                for k in (2, 3):
+                    @pl.when(inside(targets[k]))
+                    def _():
+                        pick(k)
+                        for i in (2, 1, 3, 0):
+                            send(k, i)
+        send_own(peers)
         extended[pl.ds(at, OWN)] = values[...]
 
     def shared(sems, extended, rows, first, sign):
@@ -271,7 +289,7 @@
         s01 * v0 + s11 * v1 + s12 * v2 + heat[1],
         s02 * v0 + s12 * v1 + s22 * v2 + heat[2],
     ]
-    for c, value in enumerate([s00, s11, s01, s02, s12, *work]):
+    for c, value in enumerate([s00, s01, s02, work[0], s11, s12, work[1], work[2]]):
         for s in range(SUBS):
             part_v[pl.ds((s * NUM_V + c) * OWN, OWN), :] = value[s * OWN : (s + 1) * OWN]
 
@@ -293,7 +311,15 @@
             total = total + recv[pl.ds(i * size, size), :]
         return total
 
-    reduce_to_owners(part_v, recv_v, NUM_V, 10)
+    size, part_rows = NUM_V * OWN, NUM_V * OWN // 2
+    for half in range(2):
+        for i, peer in enumerate(peers):
+            remote(
+                part_v.at[pl.ds(peer * size + half * part_rows, part_rows)],
+                recv_v.at[pl.ds(i * size + half * part_rows, part_rows)],
+                (10, 17)[half],
+                (me, peer),
+            )
 
     rho, v0, v1, v2, press = [gathered[pl.ds(v, TILES, stride=ROWS), :] for v in range(5)]
     vel = [v0, v1, v2]
@@ -313,23 +339,47 @@
 
     lax.fori_loop(0, TILES, dissipate, 0, unroll=TILES)
 
-    mixed[...] = reduced(part_v, recv_v, NUM_V, 10)
-    for r in range(OWN):
-        own_v[r] = mixed[pl.ds(r, ROWS, stride=OWN), :]
-    share(own_v, packets_v, ext_v, ROWS, 5)
-    shared(recv_sem, ext_v, ROWS, 5, -1)
+    for half, (mine, listed, extended) in enumerate(
+        [(own_v, packets_v, ext_v), (own_w, packets_w, ext_w)]
+    ):
+        drain(recv_sem, (10, 17)[half], recv_v.at[pl.ds(0, (SUBS - 1) * part_rows)])
+        total = part_v[pl.ds(sub * size + half * part_rows, part_rows), :]
+        for i in range(SUBS - 1):
+            total = total + recv_v[pl.ds(i * size + half * part_rows, part_rows), :]
+        mixed[pl.ds(half * part_rows, part_rows), :] = total
+        for r in range(OWN):
+            mine[r, pl.ds(0, 4), :] = mixed[pl.ds(half * part_rows + r, 4, stride=OWN), :]
+        share(mine, listed, extended, 4, 5 + 7 * half)
 
     def gather_v(t, carry):
         gathered_v[pl.ds(pl.multiple_of(t * ROWS, ROWS), ROWS), :] = ext_v[col_s[t]]
         return carry
 
-    lax.fori_loop(0, TILES, gather_v, 0, unroll=TILES)
-    s00, s11, s01, s02, s12, w0, w1, w2 = [
-        gathered_v[pl.ds(c, TILES, stride=ROWS), :] for c in range(NUM_V)
-    ]
-    stress = [[s00, s01, s02], [s01, s11, s12], [s02, s12, -(s00 + s11)]]
-    work = [w0, w1, w2]
+    def gather_w(t, carry):
+        gathered_w[pl.ds(pl.multiple_of(t * ROWS, ROWS), ROWS), :] = ext_w[col_s[t]]
+        return carry
+
     for d in range(3):
+        if d == 0:
+            shared(recv_sem, ext_v, 4, 5, -1)
+            lax.fori_loop(0, TILES, gather_v, 0, unroll=TILES)
+            s00, s01, s02, w0 = [gathered_v[pl.ds(c, TILES, stride=ROWS), :] for c in range(4)]
+            stress, work = [[s00, s01, s02]], [w0]
+        if d == 1:
+
+            def flux_first(t, carry):
+                at = pl.multiple_of(t * ROWS, ROWS)
+                left = fluxes[pl.ds(t, ROWS, stride=TILES), :].astype(BF16)
+                total = jnp.dot(left, weights[t, :, pl.ds(0, CELLS)], preferred_element_type=F32)
+                contribution[pl.ds(at, ROWS), :] = total - 0.1 * spread[pl.ds(at, ROWS), :]
+                return carry
+
+            lax.fori_loop(0, TILES, flux_first, 0, unroll=TILES)
+            shared(recv_sem, ext_w, 4, 12, -1)
+            lax.fori_loop(0, TILES, gather_w, 0, unroll=TILES)
+            s11, s12, w1, w2 = [gathered_w[pl.ds(c, TILES, stride=ROWS), :] for c in range(4)]
+            stress += [[s01, s11, s12], [s02, s12, -(s00 + s11)]]
+            work += [w1, w2]
         values = [mom[d]]
         for i in range(3):
             flow = mom[i] * vel[d]
@@ -343,15 +393,15 @@
     def flux(t, carry):
         at = pl.multiple_of(t * ROWS, ROWS)
         left = jnp.concatenate(
-            [fluxes[pl.ds(d * ROWS * TILES + t, ROWS, stride=TILES), :] for d in range(3)],
+            [fluxes[pl.ds(d * ROWS * TILES + t, ROWS, stride=TILES), :] for d in (1, 2)],
             axis=1,
         ).astype(BF16)
         total = jnp.dot(
             left,
-            jnp.concatenate([weights[t, :, pl.ds(d * CELLS, CELLS)] for d in range(3)], axis=0),
+            jnp.concatenate([weights[t, :, pl.ds(d * CELLS, CELLS)] for d in (1, 2)], axis=0),
             preferred_element_type=F32,
         )
-        contribution[pl.ds(at, ROWS), :] = total - 0.1 * spread[pl.ds(at, ROWS), :]
+        contribution[pl.ds(at, ROWS), :] += total
         return carry
 
     lax.fori_loop(0, TILES, flux, 0, unroll=TILES)
@@ -374,8 +424,10 @@
         out_ref[v] = base[v] - half * residual
 
     shared(send_sem, ext, 5, 0, 1)
-    drain(send_sem, 10, recv_v)
-    shared(send_sem, ext_v, ROWS, 5, 1)
+    for number in (10, 17):
+        drain(send_sem, number, recv_v.at[pl.ds(0, (SUBS - 1) * part_rows)])
+    shared(send_sem, ext_v, 4, 5, 1)
+    shared(send_sem, ext_w, 4, 12, 1)
     drain(send_sem, 11, recv_r)
 
 
@@ -410,6 +462,10 @@
             blocks(len(CURVE_STEPS) * LIST),
             blocks(SLOTS),
             row(TILES * ROWS),
+            blocks(OWN),
+            blocks(len(CURVE_STEPS) * LIST),
+            blocks(SLOTS),
+            row(TILES * ROWS),
             row(ROWS * TILES),
             row(TILES * ROWS),
             row(3 * ROWS * TILES),
@@ -422,8 +478,8 @@
             scalars(TILES),
             pltpu.SemaphoreType.DMA((CHUNKS,)),
             pltpu.SemaphoreType.DMA((7,)),
-            pltpu.SemaphoreType.DMA((12,)),
-            pltpu.SemaphoreType.DMA((12,)),
+            pltpu.SemaphoreType.DMA((18,)),
+            pltpu.SemaphoreType.DMA((18,)),
         ],
         compiler_params=pltpu.CompilerParams(
             collective_id=0, has_side_effects=True, vmem_limit_bytes=60 * 1024 * 1024

time: 39.6 us -> 39.6 us (level)
  no operation moved by 1% of the time
where the time goes in v4:
time: 39.6 us; the launch traced here: 39.4 us
  Pallas kernels  38.1 us (96%)
  local copies, waits for them, and re-layouts  1.34 us (3%)
    pallas_call x1, Pallas kernels, per_device(): pl.pallas_call(functools.partial(kernel, lax.axis_size('dom')), out_shape...  38.1 us
    unnamed x1, local copies, waits for them, and re-layouts  1.34 us

profile of v4, /device:TPU:32, one launch (start us, length us, event | category | flops | bytes accessed | tf_op | source)
XLA Modules:
  0.0 39.4 jit_solution(8624750452903124415)
XLA Ops:
  0.0 38.1 %shard_map.82 = f32[5,8,128]{2,1,0:T(8,128)} custom-call(f32[5,8,128]{2,1,0:T(8,128)} %bitcast.4, f32[5,8,128]{2,1,0:T(8,128)} %bitcast.5, f32[8,128]{1,0:T(8,128)} %ratio_h.1, s32[1,1,4,4]{3,2,1,0:T(4,128)} %send_h.1, s32[32]{0:T(128)} %row_h.1, s32[32]{0:T(128)} %col_h.1, s32[32]{0:T(128)} %flip_h.1, bf16[32,3,128,128]{3,2,1,0:T(8,128)(2,1)} %tiles_h.1), custom_call_target="tpu_custom_call" | custom-call | tf_op jit(solution)/shard_map/pallas_call | solution.py:441
  38.1 1.3 %copy.10 = f32[8,5,128]{2,0,1:T(8,128)} copy(f32[8,5,128]{2,0,1:T(8,128)} %bitcast.3) | data formatting | bytes 40960

commit v5 on v4

--- a/solution.py
+++ b/solution.py
@@ -139,45 +139,32 @@
     def drain(sems, number, like):
         pltpu.make_async_copy(like, like, sems.at[number]).wait()
 
-    def share(values, lists, extended, rows, first):
-        at = sub * OWN
-        def pick(k):
+    def share(values, lists, extended, rows, first, order):
+        def send(k):
             for j in range(LIST):
                 lists[k * LIST + j] = values[jnp.maximum(send_s[0, 0, k, j], 0)]
-
-        def send(k, i):
+            for i in (2, 1, 3, 0):
+                remote(
+                    lists.at[pl.ds(k * LIST, LIST), pl.ds(0, rows)],
+                    extended.at[pl.ds(PART + (k * SUBS + sub) * LIST, LIST), pl.ds(0, rows)],
+                    first + k,
+                    (targets[k], lax.rem(sub + i, SUBS)),
+                )
+
+        core = lax.rem(me, 2)
+        for k in order:
+            other_chip = True if k > 1 else core != k
+            pl.when(inside(targets[k]) & other_chip)(functools.partial(send, k))
+        for k in (0, 1):
+            pl.when(inside(targets[k]) & (core == k))(functools.partial(send, k))
+        for peer in peers:
             remote(
-                lists.at[pl.ds(k * LIST, LIST), pl.ds(0, rows)],
-                extended.at[pl.ds(PART + (k * SUBS + sub) * LIST, LIST), pl.ds(0, rows)],
-                first + k,
-                (targets[k], lax.rem(sub + i, SUBS)),
+                values.at[:, pl.ds(0, rows)],
+                extended.at[pl.ds(sub * OWN, OWN), pl.ds(0, rows)],
+                first + 4,
+                (me, peer),
             )
-
-        def send_own(which):
-            for peer in which:
-                remote(
-                    values.at[:, pl.ds(0, rows)],
-                    extended.at[pl.ds(at, OWN), pl.ds(0, rows)],
-                    first + 4,
-                    (me, peer),
-                )
-
-        for turn in range(2):
-            for k in (0, 1):
-                @pl.when(inside(targets[k]) & (lax.rem(me + k + turn, 2) == 1))
-                def _():
-                    pick(k)
-                    for i in (2, 1, 3, 0):
-                        send(k, i)
-            if turn == 0:
-                for k in (2, 3):
-                    @pl.when(inside(targets[k]))
-                    def _():
-                        pick(k)
-                        for i in (2, 1, 3, 0):
-                            send(k, i)
-        send_own(peers)
-        extended[pl.ds(at, OWN)] = values[...]
+        extended[pl.ds(sub * OWN, OWN)] = values[...]
 
     def shared(sems, extended, rows, first, sign):
         for k, step in enumerate(CURVE_STEPS):
@@ -208,7 +195,7 @@
         flat(own)[pl.ds(i, OWN, stride=ROWS), :] = value
 
     pl.semaphore_wait(barrier, greeted)
-    share(own, packets, ext, 5, 0)
+    share(own, packets, ext, 5, 0, (3, 1, 0, 2))
 
     for load in loads[4:]:
         load.wait()
@@ -349,7 +336,7 @@
         mixed[pl.ds(half * part_rows, part_rows), :] = total
         for r in range(OWN):
             mine[r, pl.ds(0, 4), :] = mixed[pl.ds(half * part_rows + r, 4, stride=OWN), :]
-        share(mine, listed, extended, 4, 5 + 7 * half)
+        share(mine, listed, extended, 4, 5 + 7 * half, (2, 0, 1, 3))
 
     def gather_v(t, carry):
         gathered_v[pl.ds(pl.multiple_of(t * ROWS, ROWS), ROWS), :] = ext_v[col_s[t]]

time: 39.6 us -> 39.4 us (level)
  no operation moved by 1% of the time
where the time goes in v5:
time: 39.4 us; the launch traced here: 39.3 us
  Pallas kernels  37.9 us (96%)
  local copies, waits for them, and re-layouts  1.34 us (3%)
    pallas_call x1, Pallas kernels, per_device(): pl.pallas_call(functools.partial(kernel, lax.axis_size('dom')), out_shape...  37.9 us
    unnamed x1, local copies, waits for them, and re-layouts  1.34 us

profile of v5, /device:TPU:32, one launch (start us, length us, event | category | flops | bytes accessed | tf_op | source)
XLA Modules:
  0.0 39.3 jit_solution(15758121581821303379)
XLA Ops:
  0.0 37.9 %shard_map.82 = f32[5,8,128]{2,1,0:T(8,128)} custom-call(f32[5,8,128]{2,1,0:T(8,128)} %bitcast.4, f32[5,8,128]{2,1,0:T(8,128)} %bitcast.5, f32[8,128]{1,0:T(8,128)} %ratio_h.1, s32[1,1,4,4]{3,2,1,0:T(4,128)} %send_h.1, s32[32]{0:T(128)} %row_h.1, s32[32]{0:T(128)} %col_h.1, s32[32]{0:T(128)} %flip_h.1, bf16[32,3,128,128]{3,2,1,0:T(8,128)(2,1)} %tiles_h.1), custom_call_target="tpu_custom_call" | custom-call | tf_op jit(solution)/shard_map/pallas_call | solution.py:428
  37.9 1.3 %copy.10 = f32[8,5,128]{2,0,1:T(8,128)} copy(f32[8,5,128]{2,0,1:T(8,128)} %bitcast.3) | data formatting | bytes 40960

commit v6 on v5

--- a/solution.py
+++ b/solution.py
@@ -139,7 +139,9 @@
     def drain(sems, number, like):
         pltpu.make_async_copy(like, like, sems.at[number]).wait()
 
-    def share(values, lists, extended, rows, first, order):
+    core = lax.rem(me, 2)
+
+    def share_lists(values, lists, extended, rows, first, order):
         def send(k):
             for j in range(LIST):
                 lists[k * LIST + j] = values[jnp.maximum(send_s[0, 0, k, j], 0)]
@@ -151,12 +153,10 @@
                     (targets[k], lax.rem(sub + i, SUBS)),
                 )
 
-        core = lax.rem(me, 2)
-        for k in order:
-            other_chip = True if k > 1 else core != k
-            pl.when(inside(targets[k]) & other_chip)(functools.partial(send, k))
-        for k in (0, 1):
-            pl.when(inside(targets[k]) & (core == k))(functools.partial(send, k))
+        for k, where in order:
+            pl.when(inside(targets[k]) & where)(functools.partial(send, k))
+
+    def share_own(values, extended, rows, first):
         for peer in peers:
             remote(
                 values.at[:, pl.ds(0, rows)],
@@ -165,6 +165,10 @@
                 (me, peer),
             )
         extended[pl.ds(sub * OWN, OWN)] = values[...]
+
+    later = [(2, True), (0, core == 1)]
+    earlier = [(3, True), (1, core == 0)]
+    same_chip = [(0, core == 0), (1, core == 1)]
 
     def shared(sems, extended, rows, first, sign):
         for k, step in enumerate(CURVE_STEPS):
@@ -195,7 +199,8 @@
         flat(own)[pl.ds(i, OWN, stride=ROWS), :] = value
 
     pl.semaphore_wait(barrier, greeted)
-    share(own, packets, ext, 5, 0, (3, 1, 0, 2))
+    share_lists(own, packets, ext, 5, 0, earlier + later + same_chip)
+    share_own(own, ext, 5, 0)
 
     for load in loads[4:]:
         load.wait()
@@ -326,9 +331,8 @@
 
     lax.fori_loop(0, TILES, dissipate, 0, unroll=TILES)
 
-    for half, (mine, listed, extended) in enumerate(
-        [(own_v, packets_v, ext_v), (own_w, packets_w, ext_w)]
-    ):
+    halves = [(own_v, packets_v, ext_v, 4, 5), (own_w, packets_w, ext_w, 4, 12)]
+    for half, (mine, listed, extended, rows, first) in enumerate(halves):
         drain(recv_sem, (10, 17)[half], recv_v.at[pl.ds(0, (SUBS - 1) * part_rows)])
         total = part_v[pl.ds(sub * size + half * part_rows, part_rows), :]
         for i in range(SUBS - 1):
@@ -336,7 +340,10 @@
         mixed[pl.ds(half * part_rows, part_rows), :] = total
         for r in range(OWN):
             mine[r, pl.ds(0, 4), :] = mixed[pl.ds(half * part_rows + r, 4, stride=OWN), :]
-        share(mine, listed, extended, 4, 5 + 7 * half, (2, 0, 1, 3))
+        share_lists(*halves[half], later)
+    for mine, listed, extended, rows, first in halves:
+        share_lists(mine, listed, extended, rows, first, earlier + same_chip)
+        share_own(mine, extended, rows, first)
 
     def gather_v(t, carry):
         gathered_v[pl.ds(pl.multiple_of(t * ROWS, ROWS), ROWS), :] = ext_v[col_s[t]]

time: 39.4 us -> 39.4 us (level)
  no operation moved by 1% of the time
where the time goes in v6:
time: 39.4 us; the launch traced here: 39.2 us
  Pallas kernels  37.9 us (96%)
  local copies, waits for them, and re-layouts  1.34 us (3%)
    pallas_call x1, Pallas kernels, per_device(): pl.pallas_call(functools.partial(kernel, lax.axis_size('dom')), out_shape...  37.9 us
    unnamed x1, local copies, waits for them, and re-layouts  1.34 us

profile of v6, /device:TPU:32, one launch (start us, length us, event | category | flops | bytes accessed | tf_op | source)
XLA Modules:
  0.0 39.2 jit_solution(6117742202038633395)
XLA Ops:
  0.0 37.9 %shard_map.82 = f32[5,8,128]{2,1,0:T(8,128)} custom-call(f32[5,8,128]{2,1,0:T(8,128)} %bitcast.4, f32[5,8,128]{2,1,0:T(8,128)} %bitcast.5, f32[8,128]{1,0:T(8,128)} %ratio_h.1, s32[1,1,4,4]{3,2,1,0:T(4,128)} %send_h.1, s32[32]{0:T(128)} %row_h.1, s32[32]{0:T(128)} %col_h.1, s32[32]{0:T(128)} %flip_h.1, bf16[32,3,128,128]{3,2,1,0:T(8,128)(2,1)} %tiles_h.1), custom_call_target="tpu_custom_call" | custom-call | tf_op jit(solution)/shard_map/pallas_call | solution.py:435
  37.9 1.3 %copy.10 = f32[8,5,128]{2,0,1:T(8,128)} copy(f32[8,5,128]{2,0,1:T(8,128)} %bitcast.3) | data formatting | bytes 40960

commit v7 on v6

--- a/solution.py
+++ b/solution.py
@@ -90,7 +90,7 @@
 
     barrier = pltpu.get_barrier_semaphore()
     greeted = SUBS - 1
-    for target in targets:
+    for target in [targets[k] for k in (2, 0, 3, 1)]:
         greeted = greeted + jnp.where(inside(target), SUBS, 0)
 
         @pl.when(inside(target))
@@ -141,10 +141,14 @@
 
     core = lax.rem(me, 2)
 
-    def share_lists(values, lists, extended, rows, first, order):
+    def pick(values, lists, k):
+        for j in range(LIST):
+            lists[k * LIST + j] = values[jnp.maximum(send_s[0, 0, k, j], 0)]
+
+    def share_lists(values, lists, extended, rows, first, order, picked=False):
         def send(k):
-            for j in range(LIST):
-                lists[k * LIST + j] = values[jnp.maximum(send_s[0, 0, k, j], 0)]
+            if not picked:
+                pick(values, lists, k)
             for i in (2, 1, 3, 0):
                 remote(
                     lists.at[pl.ds(k * LIST, LIST), pl.ds(0, rows)],
@@ -198,8 +202,11 @@
     ):
         flat(own)[pl.ds(i, OWN, stride=ROWS), :] = value
 
+    for k in range(len(CURVE_STEPS)):
+        pick(own, packets, k)
+
     pl.semaphore_wait(barrier, greeted)
-    share_lists(own, packets, ext, 5, 0, earlier + later + same_chip)
+    share_lists(own, packets, ext, 5, 0, earlier + later + same_chip, picked=True)
     share_own(own, ext, 5, 0)
 
     for load in loads[4:]:

time: 39.4 us -> 39.4 us (level)
  no operation moved by 1% of the time
where the time goes in v7:
time: 39.4 us; the launch traced here: 39.2 us
  Pallas kernels  37.8 us (96%)
  local copies, waits for them, and re-layouts  1.34 us (3%)
    pallas_call x1, Pallas kernels, per_device(): pl.pallas_call(functools.partial(kernel, lax.axis_size('dom')), out_shape...  37.8 us
    unnamed x1, local copies, waits for them, and re-layouts  1.34 us

profile of v7, /device:TPU:32, one launch (start us, length us, event | category | flops | bytes accessed | tf_op | source)
XLA Modules:
  0.0 39.2 jit_solution(4550226693718059415)
XLA Ops:
  0.0 37.8 %shard_map.82 = f32[5,8,128]{2,1,0:T(8,128)} custom-call(f32[5,8,128]{2,1,0:T(8,128)} %bitcast.4, f32[5,8,128]{2,1,0:T(8,128)} %bitcast.5, f32[8,128]{1,0:T(8,128)} %ratio_h.1, s32[1,1,4,4]{3,2,1,0:T(4,128)} %send_h.1, s32[32]{0:T(128)} %row_h.1, s32[32]{0:T(128)} %col_h.1, s32[32]{0:T(128)} %flip_h.1, bf16[32,3,128,128]{3,2,1,0:T(8,128)(2,1)} %tiles_h.1), custom_call_target="tpu_custom_call" | custom-call | tf_op jit(solution)/shard_map/pallas_call | solution.py:442
  37.8 1.3 %copy.10 = f32[8,5,128]{2,0,1:T(8,128)} copy(f32[8,5,128]{2,0,1:T(8,128)} %bitcast.3) | data formatting | bytes 40960

commit v8 on v3

--- a/solution.py
+++ b/solution.py
@@ -86,7 +86,7 @@
 
     barrier = pltpu.get_barrier_semaphore()
     greeted = SUBS - 1
-    for target in targets:
+    for target in [targets[k] for k in (2, 0, 3, 1)]:
         greeted = greeted + jnp.where(inside(target), SUBS, 0)
 
         @pl.when(inside(target))
@@ -135,31 +135,40 @@
     def drain(sems, number, like):
         pltpu.make_async_copy(like, like, sems.at[number]).wait()
 
-    def share(values, lists, extended, rows, first):
-        at = sub * OWN
-        for k in (2, 3, 1, 0):
-            slot = PART + (k * SUBS + sub) * LIST
-
-            @pl.when(inside(targets[k]))
-            def _():
-                for j in range(LIST):
-                    lists[k * LIST + j] = values[jnp.maximum(send_s[0, 0, k, j], 0)]
-                for i in (2, 1, 3, 0):
-                    remote(
-                        lists.at[pl.ds(k * LIST, LIST), pl.ds(0, rows)],
-                        extended.at[pl.ds(slot, LIST), pl.ds(0, rows)],
-                        first + k,
-                        (targets[k], lax.rem(sub + i, SUBS)),
-                    )
-
+    core = lax.rem(me, 2)
+
+    def pick(values, lists, k):
+        for j in range(LIST):
+            lists[k * LIST + j] = values[jnp.maximum(send_s[0, 0, k, j], 0)]
+
+    def share_lists(values, lists, extended, rows, first, order, picked=False):
+        def send(k):
+            if not picked:
+                pick(values, lists, k)
+            for i in (2, 1, 3, 0):
+                remote(
+                    lists.at[pl.ds(k * LIST, LIST), pl.ds(0, rows)],
+                    extended.at[pl.ds(PART + (k * SUBS + sub) * LIST, LIST), pl.ds(0, rows)],
+                    first + k,
+                    (targets[k], lax.rem(sub + i, SUBS)),
+                )
+
+        for k, where in order:
+            pl.when(inside(targets[k]) & where)(functools.partial(send, k))
+
+    def share_own(values, extended, rows, first):
         for peer in peers:
             remote(
                 values.at[:, pl.ds(0, rows)],
-                extended.at[pl.ds(at, OWN), pl.ds(0, rows)],
+                extended.at[pl.ds(sub * OWN, OWN), pl.ds(0, rows)],
                 first + 4,
                 (me, peer),
             )
-        extended[pl.ds(at, OWN)] = values[...]
+        extended[pl.ds(sub * OWN, OWN)] = values[...]
+
+    later = [(2, True), (0, core == 1)]
+    earlier = [(3, True), (1, core == 0)]
+    same_chip = [(0, core == 0), (1, core == 1)]
 
     def shared(sems, extended, rows, first, sign):
         for k, step in enumerate(CURVE_STEPS):
@@ -189,8 +198,12 @@
     ):
         flat(own)[pl.ds(i, OWN, stride=ROWS), :] = value
 
+    for k in range(len(CURVE_STEPS)):
+        pick(own, packets, k)
+
     pl.semaphore_wait(barrier, greeted)
-    share(own, packets, ext, 5, 0)
+    share_lists(own, packets, ext, 5, 0, earlier + later + same_chip, picked=True)
+    share_own(own, ext, 5, 0)
 
     for load in loads[4:]:
         load.wait()
@@ -316,7 +329,8 @@
     mixed[...] = reduced(part_v, recv_v, NUM_V, 10)
     for r in range(OWN):
         own_v[r] = mixed[pl.ds(r, ROWS, stride=OWN), :]
-    share(own_v, packets_v, ext_v, ROWS, 5)
+    share_lists(own_v, packets_v, ext_v, ROWS, 5, later + earlier + same_chip)
+    share_own(own_v, ext_v, ROWS, 5)
     shared(recv_sem, ext_v, ROWS, 5, -1)
 
     def gather_v(t, carry):

time: 39.6 us -> 39.5 us (level)
  no operation moved by 1% of the time
where the time goes in v8:
time: 39.5 us; the launch traced here: 39.4 us
  Pallas kernels  38 us (96%)
  local copies, waits for them, and re-layouts  1.34 us (3%)
    pallas_call x1, Pallas kernels, per_device(): pl.pallas_call(functools.partial(kernel, lax.axis_size('dom')), out_shape...  38 us
    unnamed x1, local copies, waits for them, and re-layouts  1.34 us

profile of v8, /device:TPU:32, one launch (start us, length us, event | category | flops | bytes accessed | tf_op | source)
XLA Modules:
  0.0 39.4 jit_solution(8843951526310966514)
XLA Ops:
  0.0 38.0 %shard_map.82 = f32[5,8,128]{2,1,0:T(8,128)} custom-call(f32[5,8,128]{2,1,0:T(8,128)} %bitcast.4, f32[5,8,128]{2,1,0:T(8,128)} %bitcast.5, f32[8,128]{1,0:T(8,128)} %ratio_h.1, s32[1,1,4,4]{3,2,1,0:T(4,128)} %send_h.1, s32[32]{0:T(128)} %row_h.1, s32[32]{0:T(128)} %col_h.1, s32[32]{0:T(128)} %flip_h.1, bf16[32,3,128,128]{3,2,1,0:T(8,128)(2,1)} %tiles_h.1), custom_call_target="tpu_custom_call" | custom-call | tf_op jit(solution)/shard_map/pallas_call | solution.py:403
  38.0 1.3 %copy.10 = f32[8,5,128]{2,0,1:T(8,128)} copy(f32[8,5,128]{2,0,1:T(8,128)} %bitcast.3) | data formatting | bytes 40960
